TPU v7x, 256 devices: a whole 4x4x8 slice. The times are simulated.
256 devices in a mesh: fsdp: 32 (over y, z_lo, core), tp: 8 (over z_hi, x).
Axes of the slice: x: 4, y: 4, z: 8 (z_hi: 2, z_lo: 4; z = z_hi * 4 + z_lo), core: 2. Of those that a mesh axis runs over, the one named last changes fastest.
Arguments:
- hidden_states: bfloat16 [24576, 8192], P('fsdp', 'tp'), may hold values from -6 to 6
- key_value_weight: bfloat16 [8192, 2048], P('tp'), may hold values from -0.0625 to 0.0625
- doc_lengths: int32 [32, 6], P('fsdp'), may hold values from 1 to 384, 768 in all within a row
- grad_down: float32 [256, 8192, 128], P(('fsdp', 'tp')), may hold values from -6 to 6
- grad_up: float32 [256, 1024, 128], P(('fsdp', 'tp')), may hold values from -6 to 6
- adapter_down: float32 [8, 1024, 128], P('tp', 'fsdp'), may hold values from -0.0625 to 0.0625
- first_down: float32 [8, 1024, 128], P('tp', 'fsdp'), may hold values from -3 to 3
- second_down: float32 [8, 1024, 128], P('tp', 'fsdp'), may hold values from 0.002 to 0.02
- adapter_up: float32 [1024, 128], P(('fsdp', 'tp')), may hold values from -1.5 to 1.5
- first_up: float32 [1024, 128], P(('fsdp', 'tp')), may hold values from -3 to 3
- second_up: float32 [1024, 128], P(('fsdp', 'tp')), may hold values from 0.002 to 0.02
Outputs:
- kv_states: bfloat16 [24576, 2048], P('fsdp', 'tp')
- new_down: float32 [8, 1024, 128], P('tp', 'fsdp')
- new_first_down: float32 [8, 1024, 128], P('tp', 'fsdp')
- new_second_down: float32 [8, 1024, 128], P('tp', 'fsdp')
- new_up: float32 [1024, 128], P(('fsdp', 'tp'))
- new_first_up: float32 [1024, 128], P(('fsdp', 'tp'))
- new_second_up: float32 [1024, 128], P(('fsdp', 'tp'))
Inputs may be any that keep to these rules, and one draw needn't show every extreme that they name: `doc_lengths`: each row of 6 lengths sums to 768.
All inputs are finite; a program needn't handle non-finite values.
Results may differ from a plain program's by a relative error of at most 0.018.
Values may be sent and summed in bfloat16 or wider, within the bound.
A program may use at most 64 MiB of HBM per device.

v0:
```python
import jax
import jax.numpy as jnp
from jax import lax
from jax.sharding import PartitionSpec as P

HEAD = 128


beta_one = 0.9
beta_two = 0.999
correct_one = 0.19
correct_two = 0.001999
adam_eps = 1e-08
down_learning_rate = 0.003
rate_up = 0.05
adapter_scale = 2.0
rope_base = 500000.0


def adam_step(current, moment_one, moment_two, gradient, learn_rate):
    moment_one = beta_one * moment_one + (1.0 - beta_one) * gradient
    moment_two = beta_two * moment_two + (1.0 - beta_two) * gradient * gradient
    update = moment_one / correct_one / (jnp.sqrt(moment_two / correct_two) + adam_eps)
    return (current - learn_rate * update, moment_one, moment_two)


def block_adapter(up_rows):
    column = jnp.arange(up_rows.shape[1], dtype=jnp.int32)
    is_value = (column // HEAD % 2).astype(up_rows.dtype)
    key_block = up_rows * (1 - is_value)[None, :]
    value_block = up_rows * is_value[None, :]
    return jnp.concatenate([key_block, value_block], axis=0)


def rotate(summed, lengths):
    token_count = summed.shape[0]
    doc_ends = jnp.cumsum(lengths)
    token_index = jnp.arange(token_count, dtype=jnp.int32)
    starts = jnp.sum(
        jnp.where(doc_ends[None, :] <= token_index[:, None], lengths[None, :], 0), axis=1
    )
    position = (token_index - starts).astype(jnp.float32)
    frequency = rope_base ** (-(jnp.arange(HEAD // 2, dtype=jnp.float32) * 2.0 / HEAD))
    angles = position[:, None] * frequency[None, :]
    cosine_table = jnp.cos(angles)[:, None, :]
    sine = jnp.sin(angles)[:, None, :]
    head_view = summed.reshape(token_count, -1, 2, HEAD)
    key_part = head_view[:, :, 0]
    value_part = head_view[:, :, 1]
    first_half = key_part[..., : HEAD // 2]
    second_half = key_part[..., HEAD // 2 :]
    rotated = jnp.concatenate(
        [
            first_half * cosine_table - second_half * sine,
            second_half * cosine_table + first_half * sine,
        ],
        axis=-1,
    )
    return jnp.stack([rotated, value_part], axis=2).reshape(token_count, -1)


def on_device(
    hidden_states,
    key_value_weight,
    doc_lengths,
    grad_down,
    grad_up,
    adapter_down,
    first_down,
    second_down,
    adapter_up,
    first_up,
    second_up,
):
    tile_count = lax.axis_size("tp")
    group_count = lax.axis_size("fsdp")
    local_down = grad_down[0]
    local_up = grad_up[0]
    adapter_width = local_down.shape[1]
    block_rows = local_down.shape[0] // (tile_count * group_count)
    permuted = (
        local_down.reshape(tile_count, group_count, block_rows, adapter_width)
        .transpose(1, 0, 2, 3)
        .reshape(local_down.shape)
    )
    summed_down, summed_up = (
        lax.psum_scatter(permuted, ("fsdp", "tp"), scatter_dimension=0, tiled=True),
        lax.psum_scatter(local_up, ("fsdp", "tp"), scatter_dimension=0, tiled=True),
    )
    summed_down = summed_down[None]
    new_down, new_first_down, new_second_down = adam_step(
        adapter_down, first_down, second_down, summed_down, down_learning_rate
    )
    new_up, new_first_up, new_second_up = adam_step(
        adapter_up, first_up, second_up, summed_up, rate_up
    )
    tile_down = lax.all_gather(new_down.astype(jnp.bfloat16), "fsdp", axis=1, tiled=True)[0]
    up_rows = lax.all_gather(
        new_up.astype(jnp.bfloat16), ("fsdp", "tp"), axis=0, tiled=True
    ).reshape(adapter_width // 2, -1)
    blocked = block_adapter(up_rows)
    adapter_delta = jnp.dot(tile_down, blocked, preferred_element_type=jnp.float32)
    merged_weight = (key_value_weight.astype(jnp.float32) + adapter_scale * adapter_delta).astype(
        jnp.bfloat16
    )
    partial_value = jnp.dot(hidden_states, merged_weight, preferred_element_type=jnp.float32)
    summed = lax.psum_scatter(
        partial_value.astype(jnp.bfloat16), "tp", scatter_dimension=1, tiled=True
    ).astype(jnp.float32)
    kv_states = rotate(summed, doc_lengths[0]).astype(jnp.bfloat16)
    return (
        kv_states,
        new_down,
        new_first_down,
        new_second_down,
        new_up,
        new_first_up,
        new_second_up,
    )


def solution(mesh):
    in_specs = (
        P("fsdp", "tp"),
        P("tp", None),
        P("fsdp", None),
        P(("fsdp", "tp"), None, None),
        P(("fsdp", "tp"), None, None),
        P("tp", "fsdp", None),
        P("tp", "fsdp", None),
        P("tp", "fsdp", None),
        P(("fsdp", "tp"), None),
        P(("fsdp", "tp"), None),
        P(("fsdp", "tp"), None),
    )
    out_specs = (
        P("fsdp", "tp"),
        P("tp", "fsdp", None),
        P("tp", "fsdp", None),
        P("tp", "fsdp", None),
        P(("fsdp", "tp"), None),
        P(("fsdp", "tp"), None),
        P(("fsdp", "tp"), None),
    )
    return jax.shard_map(
        on_device, mesh=mesh, in_specs=in_specs, out_specs=out_specs, check_vma=False
    )
```

profile of v0, /device:TPU:8, one launch (start us, length us, event | category | flops | bytes accessed | tf_op | source)
XLA Modules:
  0.0 1895.6 jit_solution(17184484395105095070)
XLA Ops:
  7.2 0.0 copy-start
  7.2 0.0 all-reduce.3.cloned.1.call-start
  7.2 0.7 all-reduce.3.cloned.1.call-update
  7.9 0.0 reduce-scatter.3.cloned.1.call-start
  8.0 4.8 copy.22
  12.7 0.0 copy-start.2
  12.8 0.0 copy-start.3
  12.8 0.0 reduce-scatter.3.cloned.1.call-update
  12.8 0.0 reduce-scatter.5.cloned.1.call-start
  12.9 255.5 %all-reduce.3.cloned.1.call-done = f32[1024,128]{1,0:T(8,128)} async-done(((f32[1024,128]{1,0:T(8,128)}), f32[1024,128]{1,0:T(8,128)}) %all-reduce.3.cloned.1.call-update) | async-done | bytes 524304
  268.4 0.0 copy-done.4
  268.4 0.0 copy-done.5
  268.4 0.0 copy-done.6
  268.4 1.3 convert_bitcast_fusion
  269.7 706.1 %all-gather = bf16[256,4,128]{2,1,0:T(4,128)(2,1)S(1)} all-gather(bf16[1,4,128]{2,1,0:T(4,128)(2,1)S(1)} %get-tuple-element.11), channel_id=1, replica_groups=mesh['fsdp'=32,'tp'=8] {'fsdp','tp'}, dimensions={0}, use_global_device_ids=true | all-gather | bytes 263168 | tf_op jit(solution)/shard_map/all_gather | solution.py:98
  975.8 0.2 reshape.176
  976.0 742.9 %reduce-scatter.3.cloned.1.call-done = f32[32,128]{1,0:T(8,128)} async-done(((f32[8192,128]{1,0:T(8,128)}), f32[32,128]{1,0:T(8,128)}) %reduce-scatter.3.cloned.1.call-update) | async-done | bytes 16400 | tf_op jit(solution)/shard_map/reduce_scatter | solution.py:87
  1718.9 0.0 copy-done.1
  1718.9 0.0 copy-done.2
  1718.9 0.0 copy-done.3
  1718.9 1.3 fusion.29
  1720.3 37.1 %all_gather.6 = bf16[1,1024,128]{2,1,0:T(8,128)(2,1)S(1)} all-gather(bf16[1,32,128]{2,1,0:T(8,128)(2,1)S(1)} %get-tuple-element.7), channel_id=1, replica_groups=mesh['fsdp'=32,'tp'=8] {'fsdp'}, dimensions={1}, use_global_device_ids=true | all-gather | bytes 270336 | tf_op jit(solution)/shard_map/all_gather | solution.py:97
  1757.4 0.0 copy-done
  1757.4 8.1 fusion
  1765.5 0.0 reduce-scatter.5.cloned.1.call-update
  1765.5 0.0 copy-done.7
  1765.6 0.2 reduce-window.8
  1765.7 0.1 select_reduce_fusion
  1765.8 120.3 %reduce-scatter.5.cloned.1.call-done = bf16[768,256]{0,1:T(8,128)(2,1)} async-done(((bf16[768,2048]{0,1:T(8,128)(2,1)}), bf16[768,256]{0,1:T(8,128)(2,1)}) %reduce-scatter.5.cloned.1.call-update) | async-done | bytes 393232 | tf_op jit(solution)/shard_map/reduce_scatter | solution.py:107
  1886.2 1.1 fusion.17
  1887.2 0.8 fusion.14
  1888.1 0.9 copy.24
  (12 shorter events, 0.1 us)
Async XLA Ops:
  7.2 1750.2 %copy-start = (bf16[768,1024]{1,0:T(8,128)(2,1)S(1)}, bf16[768,1024]{1,0:T(8,128)(2,1)}, u32[]{:S(2)}) copy-start(bf16[768,1024]{1,0:T(8,128)(2,1)} %param.11) | copy-start | bytes 4718596
  7.2 261.2 %all-reduce.3.cloned.1.call-start = ((), (), s32[]{:S(2)}) async-start(), calls=%async_computation.4 | async-start | bytes 1048576
  7.9 1711.0 %reduce-scatter.3.cloned.1.call-start = ((), (), s32[]{:S(2)}) async-start(), calls=%async_computation.2 | async-start | bytes 4210688 | tf_op jit(solution)/shard_map/reduce_scatter | solution.py:87
  12.7 255.7 %copy-start.4 = (f32[4,128]{1,0:T(4,128)S(1)}, f32[4,128]{1,0:T(4,128)}, u32[]{:S(2)}) copy-start(f32[4,128]{1,0:T(4,128)} %param.19) | copy-start | bytes 6148
  12.7 255.7 %copy-start.5 = (f32[4,128]{1,0:T(4,128)S(1)}, f32[4,128]{1,0:T(4,128)}, u32[]{:S(2)}) copy-start(f32[4,128]{1,0:T(4,128)} %param.20) | copy-start | bytes 6148
  12.7 255.7 %copy-start.6 = (f32[4,128]{1,0:T(4,128)S(1)}, f32[4,128]{1,0:T(4,128)}, u32[]{:S(2)}) copy-start(f32[4,128]{1,0:T(4,128)} %param.21) | copy-start | bytes 6148
  12.7 1706.2 %copy-start.1 = (f32[1,32,128]{2,1,0:T(8,128)S(1)}, f32[1,32,128]{2,1,0:T(8,128)}, u32[]{:S(2)}) copy-start(f32[1,32,128]{2,1,0:T(8,128)} %param.16) | copy-start | bytes 49156
  12.7 1706.2 %copy-start.2 = (f32[1,32,128]{2,1,0:T(8,128)S(1)}, f32[1,32,128]{2,1,0:T(8,128)}, u32[]{:S(2)}) copy-start(f32[1,32,128]{2,1,0:T(8,128)} %param.17) | copy-start | bytes 49156
  12.8 1706.1 %copy-start.3 = (f32[1,32,128]{2,1,0:T(8,128)S(1)}, f32[1,32,128]{2,1,0:T(8,128)}, u32[]{:S(2)}) copy-start(f32[1,32,128]{2,1,0:T(8,128)} %param.18) | copy-start | bytes 49156
  12.8 1873.4 %reduce-scatter.5.cloned.1.call-start = ((), (), s32[]{:S(2)}) async-start(), calls=%async_computation.3 | async-start | bytes 3538944 | tf_op jit(solution)/shard_map/reduce_scatter | solution.py:107
  1757.4 8.2 copy-start.7
Sparse Core Ops, SparseCore 0:
  13.5 254.8 all-reduce.2
  270.9 1447.9 reduce-scatter.2
  1765.7 120.4 reduce-scatter.4
where the time goes:
time: 1900 us
  waiting for transfers between devices  1120 us (59%)
  blocking collectives  743 us (39%)
    reduce_scatter x1, waiting for transfers between devices, on_device(): lax.psum_scatter(permuted, ('fsdp', 'tp'), scatter_dimension=0, tiled=True)  743 us
    all_gather x1, blocking collectives, on_device(): lax.all_gather(new_up.astype(jnp.bfloat16), ('fsdp', 'tp'), axis=0, tiled...  706 us
    unnamed x4, waiting for transfers between devices  256 us
    reduce_scatter x1, waiting for transfers between devices, on_device(): lax.psum_scatter(partial_value.astype(jnp.bfloat16), 'tp', scatter_dimens...  120 us
  transfers between devices with their start and end apart: 3, of which 3 were waited for; matrix products, arithmetic and copies ran while one was open for 0% of the time, Pallas kernels for 0%

commit v1 on v0

v1 whole, which is shorter than its diff:
```python
import jax
import jax.numpy as jnp
from jax import lax
from jax.experimental import pallas as pl
from jax.experimental.pallas import tpu as pltpu
from jax.sharding import PartitionSpec as P

HEAD = 128
TOKENS_LOCAL = 768
FEATURES = 1024
HEAD_COLUMNS = 256
PIECE = 48
MESH = pl.DeviceIdType.MESH

beta_one = 0.9
beta_two = 0.999
correct_one = 0.19
correct_two = 0.001999
adam_eps = 1e-08
down_learning_rate = 0.003
rate_up = 0.05
adapter_scale = 2.0
rope_base = 500000.0

Z_STEPS = (2, 1, 3, 0)
X_STEPS = (2, 1, 3, 0)


def adam_step(current, moment_one, moment_two, gradient, learn_rate):
    moment_one = beta_one * moment_one + (1.0 - beta_one) * gradient
    moment_two = beta_two * moment_two + (1.0 - beta_two) * gradient * gradient
    update = moment_one / correct_one / (jnp.sqrt(moment_two / correct_two) + adam_eps)
    return (current - learn_rate * update, moment_one, moment_two)


def dot(a, b):
    return jnp.dot(a, b, preferred_element_type=jnp.float32)


def kernel(
    hidden, weight, lengths, grad_down, grad_up, p_down, m_down, v_down, p_up, m_up, v_up,
    out, new_p_down, new_m_down, new_v_down, new_p_up, new_m_up, new_v_up,
    hid, wv, gv, cs, cr, ys, yr, zs, zr, ab, hs, hr, hall, xs, xr, own_heads, zbs, zbr,
    table, state, up_state, up_all, new_down_v, new_up_v, out_v,
    ld_sem, core_s, core_r, y_s, y_r, z_s, z_r, a_s, a_r, f_s, f_r, hs_s, hs_r, hg_s, hg_r,
    x_s, x_r, b_s, b_r, u_s, u_r, st_sem, o_sem,
):
    f = lax.axis_index("fsdp")
    t = lax.axis_index("tp")
    y, zl, c, zh, x = f // 8, (f // 2) % 4, f % 2, t // 4, t % 4
    chip = f // 2

    def f_of(y_, zl_, c_):
        return (y_ * 4 + zl_) * 2 + c_

    barrier = pltpu.get_barrier_semaphore()
    partners = [(f_of(y, zl, 1 - c), t)]
    for k in range(1, 16):
        q = (chip + k) % 16
        partners.append((q * 2 + c, t))
    for dz in range(4):
        for k in range(8):
            if k == 0:
                continue
            partners.append((f_of(y, (zl + dz) % 4, c), (t + k) % 8))
    for p in partners:
        pl.semaphore_signal(barrier, inc=1, device_id=p, device_id_type=MESH)

    heads = []
    for half in range(2):
        for dx in X_STEPS:
            zh_ = (1 - zh) if half == 0 else zh
            heads.append((half, dx, zh_ * 4 + (x + dx) % 4))
    loads = {}

    def load(name, src, dst):
        i = len(loads)
        cp = pltpu.make_async_copy(src, dst, ld_sem.at[i])
        cp.start()
        loads[name] = cp

    def load_grad(j):
        z_ = (zl + Z_STEPS[j]) % 4
        load(("d", j), grad_down.at[:, :, z_], gv.at[j, pl.ds(0, 8)])
        load(("u", j), grad_up.at[:, z_], gv.at[j, 8])

    def load_head(i):
        col = pl.multiple_of(heads[i][2] * HEAD_COLUMNS, HEAD_COLUMNS)
        load(("w", i), weight.at[:, pl.ds(col, HEAD_COLUMNS)], wv.at[i])

    load_grad(0)
    load("hid", hidden, hid)
    load_head(0)
    load_grad(1)
    load_head(1)
    load_grad(2)
    load_head(2)
    load_grad(3)
    for i in range(3, 8):
        load_head(i)
    load("p", p_down, state.at[0])
    load("m", m_down, state.at[1])
    load("v", v_down, state.at[2])
    up_state[...] = jnp.zeros_like(up_state)
    load("pu", p_up, up_state.at[pl.ds(0, 4)])
    load("mu", m_up, up_state.at[pl.ds(8, 4)])
    load("vu", v_up, up_state.at[pl.ds(16, 4)])

    copies = []

    def send(src, dst, ss, rs, to):
        cp = pltpu.make_async_remote_copy(
            src_ref=src, dst_ref=dst, send_sem=ss, recv_sem=rs, device_id=to, device_id_type=MESH
        )
        cp.start()
        return cp

    def await_recv(ref, sem):
        pltpu.make_async_copy(ref, ref, sem).wait()

    def phase_a(j):
        loads[("d", j)].wait()
        loads[("u", j)].wait()

        @pl.loop(0, 4)
        def _(k):
            cs[j, k] = gv[j, :, (y + k) % 4, 1 - c].astype(jnp.bfloat16)

        if j == 0:
            pl.semaphore_wait(barrier, len(partners))
        copies.append(send(cs.at[j], cr.at[j], core_s.at[j], core_r.at[j], (f_of(y, zl, 1 - c), t)))

    def phase_b(j):
        await_recv(cr.at[j], core_r.at[j])
        for k in (2, 1, 3):
            ys[j, k - 1] = (
                gv[j, :, (y + k) % 4, c] + cr[j, k].astype(jnp.float32)
            ).astype(jnp.bfloat16)
            copies.append(
                send(
                    ys.at[j, k - 1], yr.at[j, k - 1], y_s.at[j, k - 1], y_r.at[j, k - 1],
                    (f_of((y + k) % 4, zl, c), t),
                )
            )

    rows = lax.broadcasted_iota(jnp.int32, (128, 32), 0)
    cols = lax.broadcasted_iota(jnp.int32, (128, 32), 1)
    tile, r = rows // 16, rows % 16
    wanted = jnp.where(
        r < 4, 4 * tile + r, jnp.where(r < 6, 2 * tile + r - 4, 2 * tile + r + 10)
    )
    pick = jnp.where((wanted == cols) & (r < 8), 1.0, 0.0).astype(jnp.bfloat16)

    def phase_c(j):
        for k in range(3):
            await_recv(yr.at[j, k], y_r.at[j, k])
        total = (
            gv[j, :, y, c]
            + cr[j, 0].astype(jnp.float32)
            + yr[j, 0].astype(jnp.float32)
            + yr[j, 1].astype(jnp.float32)
            + yr[j, 2].astype(jnp.float32)
        ).astype(jnp.bfloat16)
        zs[j, :, 0:32] = total[0:8]
        zs[j, :, 32:48] = dot(pick, total[8]).astype(jnp.bfloat16).reshape(8, 16, 128)
        to_f = f_of(y, (zl + Z_STEPS[j]) % 4, c)
        for k in range(8):
            if Z_STEPS[j] == 0 and k == 0:
                continue
            to_t = (t + k) % 8
            send(zs.at[j, to_t], zr.at[j, k], z_s.at[j], z_r.at[j], (to_f, to_t))

    def up_exchange():
        for name in ("pu", "mu", "vu"):
            loads[name].wait()
        up_all[t] = up_state[...]
        for k in range(1, 8):
            send(up_state, up_all.at[t], u_s, u_r, (f, (t + k) % 8))

    def head(i):
        half, dx, _ = heads[i]
        loads[("w", i)].wait()
        slot = half * 3 + X_STEPS.index(dx)

        @pl.loop(0, 3)
        def _(m):
            part = pl.ds(pl.multiple_of(m * 256, 256), 256)
            value = dot(hid[part, :], wv[i])
            if dx == 0:
                own_heads[half, part, :] = value
            else:
                xs[slot, part, :] = value.astype(jnp.bfloat16)

        if dx != 0:
            copies.append(
                send(xs.at[slot], xr.at[slot], x_s.at[slot], x_r.at[slot], (f, zh * 4 + (x + dx) % 4))
            )

    def head_forward():
        for s in range(3):
            await_recv(xr.at[s], x_r.at[s])

        @pl.loop(0, 6)
        def _(m):
            part = pl.ds(pl.multiple_of(m * 128, 128), 128)
            zbs[part, :] = (
                own_heads[0, part, :]
                + xr[0, part, :].astype(jnp.float32)
                + xr[1, part, :].astype(jnp.float32)
                + xr[2, part, :].astype(jnp.float32)
            ).astype(jnp.bfloat16)

        copies.append(send(zbs, zbr, b_s, b_r, (f, (1 - zh) * 4 + x)))

    def trig():
        lane = lax.broadcasted_iota(jnp.int32, (128, 128), 1)
        freq = jnp.exp(
            (lane % 64).astype(jnp.float32) * (-2.0 / HEAD * 13.122363377404328)
        )
        shift = jnp.where(lane < 64, 0.5 * 3.141592653589793, 0.0)

        @pl.loop(0, 6)
        def _(m):
            index = lax.broadcasted_iota(jnp.int32, (128, 128), 0) + m * 128
            start = jnp.zeros((128, 128), jnp.int32)
            end = jnp.int32(0)
            for d in range(6):
                end = end + lengths[0, d]
                start = start + jnp.where(index >= end, lengths[0, d], 0)
            angle = (index - start).astype(jnp.float32) * freq
            table[pl.ds(pl.multiple_of(m * 128, 128), 128), :] = jnp.sin(angle + shift)

    phase_a(0)
    loads["hid"].wait()
    head(0)
    phase_a(1)
    phase_b(0)
    head(1)
    phase_a(2)
    phase_b(1)
    head(2)
    phase_a(3)
    phase_b(2)
    head(4)
    phase_b(3)
    phase_c(0)
    head(5)
    phase_c(1)
    head(6)
    up_exchange()
    phase_c(2)
    head(3)
    phase_c(3)
    head(7)
    trig()

    for j in range(3):
        await_recv(zr.at[j], z_r.at[j])
    await_recv(zr.at[3, pl.ds(1, 7)], z_r.at[3])
    total = zs[3, t].astype(jnp.float32)
    for j in range(4):
        for k in range(8):
            if j == 3 and k == 0:
                continue
            total = total + zr[j, k].astype(jnp.float32)
    for name in ("p", "m", "v"):
        loads[name].wait()
    new = adam_step(state[0], state[1], state[2], total[0:32], down_learning_rate)
    ab[chip, c, 0:32] = new[0].astype(jnp.bfloat16)
    await_recv(up_all.at[pl.ds(0, 7)], u_r)
    first, second = up_all[t // 2], up_all[4 + t // 2]
    odd = t % 2 == 1

    def of_head(row):
        return jnp.concatenate(
            [
                jnp.where(odd, first[row + 2 : row + 4], first[row : row + 2]),
                jnp.where(odd, second[row + 2 : row + 4], second[row : row + 2]),
            ],
            axis=0,
        )

    new_head = adam_step(of_head(0), of_head(8), of_head(16), total[36:40], rate_up)[0]
    ab[chip, c, 32:48] = jnp.concatenate(
        [new_head, jnp.zeros((12, 128), jnp.float32)], axis=0
    ).astype(jnp.bfloat16)
    for k in range(1, 16):
        q = (chip + k) % 16
        send(ab.at[chip, c], ab.at[chip, c], a_s, a_r, (q * 2 + c, t))
    new_up = adam_step(
        up_state[0:4], up_state[8:12], up_state[16:20], total[32:36], rate_up
    )
    outs = []
    for n, ref in enumerate((new_p_down, new_m_down, new_v_down)):
        new_down_v[n] = new[n]
        outs.append(pltpu.make_async_copy(new_down_v.at[n], ref, o_sem.at[n]))
    for n, ref in enumerate((new_p_up, new_m_up, new_v_up)):
        new_up_v[n] = new_up[n]
        outs.append(pltpu.make_async_copy(new_up_v.at[n], ref, o_sem.at[3 + n]))
    for cp in outs:
        cp.start()

    await_recv(ab.at[pl.ds(0, 15), c], a_r)
    copies.append(send(ab.at[:, c], ab.at[:, c], f_s, f_r, (f_of(y, zl, 1 - c), t)))
    head_forward()
    await_recv(ab.at[:, 1 - c], f_r)

    adapter = ab[:, :, 0:32].reshape(FEATURES, 128)
    for k in (4, 5, 3, 6, 2, 7, 1, 0):
        to_t = (t + k) % 8
        part = pl.ds(pl.multiple_of(to_t * 96, 96), 96)
        hs[to_t] = dot(hid[part, :], adapter).astype(jnp.bfloat16)
        if k:
            send(hs.at[to_t], hr.at[k - 1], hs_s, hs_r, (f, to_t))
    select_row = lax.broadcasted_iota(jnp.int32, (128, 512), 0)
    select_col = lax.broadcasted_iota(jnp.int32, (128, 512), 1)
    place = (select_row % 64) // 2 * 16 + select_row % 2 * 2
    key_pick = jnp.where((select_row < 64) & (select_col == place), 1.0, 0.0)
    value_pick = jnp.where((select_row >= 64) & (select_col == place + 1), 1.0, 0.0)
    rolls = ab[:, :, 32:48].reshape(512, 128)
    key_block = dot(key_pick.astype(jnp.bfloat16), rolls).astype(jnp.bfloat16)
    value_block = dot(value_pick.astype(jnp.bfloat16), rolls).astype(jnp.bfloat16)

    await_recv(hr, hs_r)
    mixed = hs[t].astype(jnp.float32)
    for k in range(7):
        mixed = mixed + hr[k].astype(jnp.float32)
    hall[t] = mixed.astype(jnp.bfloat16)
    for k in (4, 5, 3, 6, 2, 7, 1):
        send(hall.at[t], hall.at[t], hg_s, hg_r, (f, (t + k) % 8))

    for s in range(3, 6):
        await_recv(xr.at[s], x_r.at[s])
    await_recv(zbr, b_r)

    @pl.loop(0, 6)
    def _(m):
        part = pl.ds(pl.multiple_of(m * 128, 128), 128)
        own_heads[1, part, :] = (
            own_heads[1, part, :]
            + xr[3, part, :].astype(jnp.float32)
            + xr[4, part, :].astype(jnp.float32)
            + xr[5, part, :].astype(jnp.float32)
            + zbr[part, :].astype(jnp.float32)
        )

    await_recv(hall.at[pl.ds(0, 7)], hg_r)
    final = []
    low = lax.broadcasted_iota(jnp.int32, (96, 128), 1) < 64
    for m in range(8):
        part = pl.ds(m * 96, 96)
        rot = table[part, :]
        swapped = pltpu.roll(rot, 64, 1)
        cosine = jnp.where(low, rot, swapped)
        sine = jnp.where(low, -swapped, rot)
        key = own_heads[1, part, 0:128] + adapter_scale * dot(hall[m], key_block)
        value = own_heads[1, part, 128:256] + adapter_scale * dot(hall[m], value_block)
        out_v[part, 0:128] = (key * cosine + pltpu.roll(key, 64, 1) * sine).astype(jnp.bfloat16)
        out_v[part, 128:256] = value.astype(jnp.bfloat16)
    last = pltpu.make_async_copy(out_v, out, st_sem)
    last.start()

    for cp in copies:
        cp.wait_send()
    for j in range(3):
        await_recv(zs.at[j], z_s.at[j])
    await_recv(zs.at[3, pl.ds(1, 7)], z_s.at[3])
    await_recv(up_all.at[pl.ds(0, 7)], u_s)
    await_recv(ab.at[pl.ds(0, 15), c], a_s)
    await_recv(hr, hs_s)
    await_recv(hr, hg_s)
    for cp in outs:
        cp.wait()
    last.wait()


def on_device(
    hidden_states, key_value_weight, doc_lengths, grad_down, grad_up,
    adapter_down, first_down, second_down, adapter_up, first_up, second_up,
):
    bf16, f32 = jnp.bfloat16, jnp.float32
    anywhere = pl.BlockSpec(memory_space=pl.ANY)
    vm = pltpu.VMEM
    dma = pltpu.SemaphoreType.DMA
    results = pl.pallas_call(
        kernel,
        out_shape=[jax.ShapeDtypeStruct((TOKENS_LOCAL, HEAD_COLUMNS), bf16)]
        + [jax.ShapeDtypeStruct((32, 128), f32)] * 3
        + [jax.ShapeDtypeStruct((4, 128), f32)] * 3,
        in_specs=[anywhere, anywhere, pl.BlockSpec(memory_space=pltpu.SMEM)] + [anywhere] * 8,
        out_specs=[anywhere] * 7,
        scratch_shapes=[
            vm((TOKENS_LOCAL, FEATURES), bf16),
            vm((8, FEATURES, HEAD_COLUMNS), bf16),
            vm((4, 9, 4, 2, 32, 128), f32),
            vm((4, 4, 9, 32, 128), bf16),
            vm((4, 4, 9, 32, 128), bf16),
            vm((4, 3, 9, 32, 128), bf16),
            vm((4, 3, 9, 32, 128), bf16),
            vm((4, 8, PIECE, 128), bf16),
            vm((4, 8, PIECE, 128), bf16),
            vm((16, 2, PIECE, 128), bf16),
            vm((8, 96, 128), bf16),
            vm((7, 96, 128), bf16),
            vm((8, 96, 128), bf16),
            vm((6, TOKENS_LOCAL, HEAD_COLUMNS), bf16),
            vm((6, TOKENS_LOCAL, HEAD_COLUMNS), bf16),
            vm((2, TOKENS_LOCAL, HEAD_COLUMNS), f32),
            vm((TOKENS_LOCAL, HEAD_COLUMNS), bf16),
            vm((TOKENS_LOCAL, HEAD_COLUMNS), bf16),
            vm((TOKENS_LOCAL, 128), f32),
            vm((3, 32, 128), f32),
            vm((24, 128), f32),
            vm((8, 24, 128), f32),
            vm((3, 32, 128), f32),
            vm((3, 4, 128), f32),
            vm((TOKENS_LOCAL, HEAD_COLUMNS), bf16),
            dma((24,)),
            dma((4,)), dma((4,)),
            dma((4, 3)), dma((4, 3)),
            dma((4,)), dma((4,)),
            dma(()), dma(()),
            dma(()), dma(()),
            dma(()), dma(()),
            dma(()), dma(()),
            dma((6,)), dma((6,)),
            dma(()), dma(()),
            dma(()), dma(()),
            dma(()),
            dma((6,)),
        ],
        compiler_params=pltpu.CompilerParams(
            collective_id=0, has_side_effects=True, vmem_limit_bytes=56 * 1024 * 1024
        ),
        cost_estimate=pl.CostEstimate(
            flops=2 * TOKENS_LOCAL * FEATURES * 2200, bytes_accessed=12 << 20, transcendentals=0
        ),
    )(
        hidden_states,
        key_value_weight,
        doc_lengths,
        grad_down.reshape(8, 4, 4, 2, 32, 128),
        grad_up.reshape(4, 4, 2, 32, 128),
        adapter_down[0],
        first_down[0],
        second_down[0],
        adapter_up,
        first_up,
        second_up,
    )
    states, p_down, m_down, v_down, p_up, m_up, v_up = results
    return (states, p_down[None], m_down[None], v_down[None], p_up, m_up, v_up)


def solution(mesh):
    matrix = P(("fsdp", "tp"), None)
    down = P("tp", "fsdp", None)
    partial = P(("fsdp", "tp"), None, None)
    in_specs = (
        P("fsdp", "tp"), P("tp", None), P("fsdp", None), partial, partial,
        down, down, down, matrix, matrix, matrix,
    )
    out_specs = (P("fsdp", "tp"), down, down, down, matrix, matrix, matrix)
    return jax.shard_map(
        on_device, mesh=mesh, in_specs=in_specs, out_specs=out_specs, check_vma=False
    )
```

time: 1900 us -> 105 us (0.06)
  waiting for transfers between devices: 1120 us -> 0 us
  blocking collectives: 743 us -> 0 us
  Pallas kernels: 0 us -> 94.1 us
    reduce_scatter x2 -> x0, waiting for transfers between devices: 863 us -> none  [the longest x1 743 us: on_device(): lax.psum_scatter(permuted, ('fsdp', 'tp'), scatter_dimension=0, tiled=True)]
    all_gather x2 -> x0, blocking collectives: 743 us -> none  [the longest x1 706 us: on_device(): lax.all_gather(new_up.astype(jnp.bfloat16), ('fsdp', 'tp'), axis=0, tiled...]
    unnamed x4 -> x0, waiting for transfers between devices: 256 us -> none
    pallas_call x0 -> x1, Pallas kernels: none -> 94.1 us  [on_device(): pl.pallas_call(kernel, out_shape=[jax.ShapeDtypeStruct((TOKENS_LOCAL, HEA...]
  transfers between devices with their start and end apart: 3 -> 0, of which waited for: 3 -> 0; matrix products, arithmetic and copies ran while one was open for 0% -> 0% of each run, Pallas kernels for 0% -> 0%
where the time goes in v1:
time: 105 us; the launch traced here: 104 us
  Pallas kernels  94.1 us (90%)
  local copies, waits for them, and re-layouts  9.49 us (9%)
    pallas_call x1, Pallas kernels, on_device(): pl.pallas_call(kernel, out_shape=[jax.ShapeDtypeStruct((TOKENS_LOCAL, HEA...  94.1 us
    unnamed x7, local copies, waits for them, and re-layouts  9.49 us

profile of v1, /device:TPU:8, one launch (start us, length us, event | category | flops | bytes accessed | tf_op | source)
XLA Modules:
  0.0 104.2 jit_solution(6445380238665059879)
XLA Ops:
  0.6 94.1 %shard_map.162 = (bf16[768,256]{1,0:T(8,128)(2,1)}, f32[32,128]{1,0:T(8,128)}, f32[32,128]{1,0:T(8,128)}, f32[32,128]{1,0:T(8,128)}, f32[4,128]{1,0:T(4,128)}, /*index=5*/f32[4,128]{1,0:T(4,128)}, f32[4,128]{1,0:T(4,128)}) custom-call(bf16[768,1024]{1,0:T(8,128)(2,1)} %hidden.1, bf16[1024,2048]{1,0:T(8,128)(2,1)} %weight.1, s32[1,6]{1,0:T(1,128)} %lengths.1, ...), custom_call_target="tpu_custom_call" | custom-call | flops 3460300800 | bytes 12582912 | tf_op jit(solution)/shard_map/pallas_call | solution.py:385
  94.7 1.8 %copy.25 = bf16[768,256]{1,0:T(8,128)(2,1)} copy(bf16[768,256]{1,0:T(8,128)(2,1)} %get-tuple-element.28) | data formatting | bytes 786432
  96.5 1.3 %copy.26 = f32[1,32,128]{2,1,0:T(8,128)} copy(f32[1,32,128]{2,1,0:T(8,128)} %bitcast.10) | data formatting | bytes 32768
  97.8 1.3 %copy.27 = f32[1,32,128]{2,1,0:T(8,128)} copy(f32[1,32,128]{2,1,0:T(8,128)} %bitcast.9) | data formatting | bytes 32768
  99.1 1.3 %copy.28 = f32[1,32,128]{2,1,0:T(8,128)} copy(f32[1,32,128]{2,1,0:T(8,128)} %bitcast.8) | data formatting | bytes 32768
  100.4 1.3 %copy.29 = f32[4,128]{1,0:T(4,128)} copy(f32[4,128]{1,0:T(4,128)} %get-tuple-element.32) | data formatting | bytes 4096
  101.7 1.3 %copy.30 = f32[4,128]{1,0:T(4,128)} copy(f32[4,128]{1,0:T(4,128)} %get-tuple-element.33) | data formatting | bytes 4096
  103.0 1.2 %copy.31 = f32[4,128]{1,0:T(4,128)} copy(f32[4,128]{1,0:T(4,128)} %get-tuple-element.34) | data formatting | bytes 4096

commit v2 on v1

--- a/solution.py
+++ b/solution.py
@@ -39,11 +39,11 @@
 
 def kernel(
     hidden, weight, lengths, grad_down, grad_up, p_down, m_down, v_down, p_up, m_up, v_up,
-    out, new_p_down, new_m_down, new_v_down, new_p_up, new_m_up, new_v_up,
-    hid, wv, gv, cs, cr, ys, yr, zs, zr, ab, hs, hr, hall, xs, xr, own_heads, zbs, zbr,
-    table, state, up_state, up_all, new_down_v, new_up_v, out_v,
+    out_h, new_down_h, new_up_h,
+    hid, wv, gv, cs, cr, ys, yr, zs, zr, ab, hs, hr, hall, far, mid, near, near_b, xr, own_heads, zbs, zbr,
+    table, state, up_state, up_all, out_v, new_down_v, new_up_v,
     ld_sem, core_s, core_r, y_s, y_r, z_s, z_r, a_s, a_r, f_s, f_r, hs_s, hs_r, hg_s, hg_r,
-    x_s, x_r, b_s, b_r, u_s, u_r, st_sem, o_sem,
+    far_s, far_r, x_s, x_r, b_s, b_r, u_s, u_r, o_sem,
 ):
     f = lax.axis_index("fsdp")
     t = lax.axis_index("tp")
@@ -89,14 +89,12 @@
         load(("w", i), weight.at[:, pl.ds(col, HEAD_COLUMNS)], wv.at[i])
 
     load_grad(0)
+    load_grad(1)
     load("hid", hidden, hid)
     load_head(0)
-    load_grad(1)
-    load_head(1)
     load_grad(2)
-    load_head(2)
     load_grad(3)
-    for i in range(3, 8):
+    for i in range(1, 8):
         load_head(i)
     load("p", p_down, state.at[0])
     load("m", m_down, state.at[1])
@@ -106,17 +104,15 @@
     load("mu", m_up, up_state.at[pl.ds(8, 4)])
     load("vu", v_up, up_state.at[pl.ds(16, 4)])
 
-    copies = []
-
     def send(src, dst, ss, rs, to):
-        cp = pltpu.make_async_remote_copy(
+        pltpu.make_async_remote_copy(
             src_ref=src, dst_ref=dst, send_sem=ss, recv_sem=rs, device_id=to, device_id_type=MESH
-        )
-        cp.start()
-        return cp
-
-    def await_recv(ref, sem):
+        ).start()
+
+    def await_bytes(ref, sem):
         pltpu.make_async_copy(ref, ref, sem).wait()
+
+    sent = []
 
     def phase_a(j):
         loads[("d", j)].wait()
@@ -126,22 +122,21 @@
         def _(k):
             cs[j, k] = gv[j, :, (y + k) % 4, 1 - c].astype(jnp.bfloat16)
 
-        if j == 0:
-            pl.semaphore_wait(barrier, len(partners))
-        copies.append(send(cs.at[j], cr.at[j], core_s.at[j], core_r.at[j], (f_of(y, zl, 1 - c), t)))
+    def core_send(j):
+        send(cs.at[j], cr.at[j], core_s.at[j], core_r.at[j], (f_of(y, zl, 1 - c), t))
+        sent.append((cs.at[j], core_s.at[j]))
 
     def phase_b(j):
-        await_recv(cr.at[j], core_r.at[j])
+        await_bytes(cr.at[j], core_r.at[j])
         for k in (2, 1, 3):
             ys[j, k - 1] = (
                 gv[j, :, (y + k) % 4, c] + cr[j, k].astype(jnp.float32)
             ).astype(jnp.bfloat16)
-            copies.append(
-                send(
-                    ys.at[j, k - 1], yr.at[j, k - 1], y_s.at[j, k - 1], y_r.at[j, k - 1],
-                    (f_of((y + k) % 4, zl, c), t),
-                )
+            send(
+                ys.at[j, k - 1], yr.at[j, k - 1], y_s.at[j, k - 1], y_r.at[j, k - 1],
+                (f_of((y + k) % 4, zl, c), t),
             )
+            sent.append((ys.at[j, k - 1], y_s.at[j, k - 1]))
 
     rows = lax.broadcasted_iota(jnp.int32, (128, 32), 0)
     cols = lax.broadcasted_iota(jnp.int32, (128, 32), 1)
@@ -153,7 +148,7 @@
 
     def phase_c(j):
         for k in range(3):
-            await_recv(yr.at[j, k], y_r.at[j, k])
+            await_bytes(yr.at[j, k], y_r.at[j, k])
         total = (
             gv[j, :, y, c]
             + cr[j, 0].astype(jnp.float32)
@@ -169,6 +164,7 @@
                 continue
             to_t = (t + k) % 8
             send(zs.at[j, to_t], zr.at[j, k], z_s.at[j], z_r.at[j], (to_f, to_t))
+        sent.append((zs.at[j] if Z_STEPS[j] else zs.at[j, pl.ds(1, 7)], z_s.at[j]))
 
     def up_exchange():
         for name in ("pu", "mu", "vu"):
@@ -176,41 +172,83 @@
         up_all[t] = up_state[...]
         for k in range(1, 8):
             send(up_state, up_all.at[t], u_s, u_r, (f, (t + k) % 8))
-
-    def head(i):
-        half, dx, _ = heads[i]
+        sent.append((up_all.at[pl.ds(0, 7)], u_s))
+
+    upper, lower = pl.ds(0, 384), pl.ds(384, 384)
+    x_next, x_prev = (f, zh * 4 + (x + 1) % 4), (f, zh * 4 + (x + 3) % 4)
+
+    def product(i, place):
         loads[("w", i)].wait()
-        slot = half * 3 + X_STEPS.index(dx)
 
         @pl.loop(0, 3)
         def _(m):
             part = pl.ds(pl.multiple_of(m * 256, 256), 256)
-            value = dot(hid[part, :], wv[i])
-            if dx == 0:
-                own_heads[half, part, :] = value
-            else:
-                xs[slot, part, :] = value.astype(jnp.bfloat16)
-
-        if dx != 0:
-            copies.append(
-                send(xs.at[slot], xr.at[slot], x_s.at[slot], x_r.at[slot], (f, zh * 4 + (x + dx) % 4))
-            )
+            place[part, :] = dot(hid[part, :], wv[i]).astype(place.dtype)
+
+    def far_head(half):
+        product(half * 4, far.at[half])
+
+    def far_send(half):
+        send(far.at[half, upper], mid.at[half, 0], far_s.at[half, 0], far_r.at[half, 0], x_next)
+        send(far.at[half, lower], mid.at[half, 1], far_s.at[half, 1], far_r.at[half, 1], x_prev)
+        sent.append((far.at[half, upper], far_s.at[half, 0]))
+        sent.append((far.at[half, lower], far_s.at[half, 1]))
+
+    def near_head(half, side):
+        product(half * 4 + 1 + side, near.at[side])
+        mine = lower if side == 0 else upper
+
+        @pl.loop(0, 3)
+        def _(m):
+            part = pl.ds(pl.multiple_of((384 if side == 0 else 0) + m * 128, 128), 128)
+            near_b[half, side, part, :] = near[side, part, :].astype(jnp.bfloat16)
+
+        send(
+            near_b.at[half, side, mine], xr.at[half, side, mine], x_s.at[half, side, 0], x_r.at[half, side, 0],
+            x_next if side == 0 else x_prev,
+        )
+        sent.append((near_b.at[half, side, mine], x_s.at[half, side, 0]))
+
+    def near_sum(half, side):
+        await_bytes(mid.at[half, side], far_r.at[half, side])
+        mine = upper if side == 0 else lower
+
+        @pl.loop(0, 3)
+        def _(m):
+            local = pl.ds(pl.multiple_of(m * 128, 128), 128)
+            part = pl.ds(pl.multiple_of((0 if side == 0 else 384) + m * 128, 128), 128)
+            near_b[half, side, part, :] = (
+                near[side, part, :] + mid[half, side, local, :].astype(jnp.float32)
+            ).astype(jnp.bfloat16)
+
+        send(
+            near_b.at[half, side, mine], xr.at[half, side, mine], x_s.at[half, side, 1], x_r.at[half, side, 1],
+            x_next if side == 0 else x_prev,
+        )
+        sent.append((near_b.at[half, side, mine], x_s.at[half, side, 1]))
+
+    def own_head(half):
+        product(half * 4 + 3, own_heads.at[half])
+
+    def head_arrive(half):
+        for side in range(2):
+            await_bytes(xr.at[half, side, lower], x_r.at[half, side, 0])
+            await_bytes(xr.at[half, side, upper], x_r.at[half, side, 1])
 
     def head_forward():
-        for s in range(3):
-            await_recv(xr.at[s], x_r.at[s])
+        head_arrive(0)
 
         @pl.loop(0, 6)
         def _(m):
             part = pl.ds(pl.multiple_of(m * 128, 128), 128)
             zbs[part, :] = (
                 own_heads[0, part, :]
-                + xr[0, part, :].astype(jnp.float32)
-                + xr[1, part, :].astype(jnp.float32)
-                + xr[2, part, :].astype(jnp.float32)
+                + xr[0, 0, part, :].astype(jnp.float32)
+                + xr[0, 1, part, :].astype(jnp.float32)
             ).astype(jnp.bfloat16)
 
-        copies.append(send(zbs, zbr, b_s, b_r, (f, (1 - zh) * 4 + x)))
+        send(zbs, zbr, b_s, b_r, (f, (1 - zh) * 4 + x))
+        sent.append((zbs, b_s))
 
     def trig():
         lane = lax.broadcasted_iota(jnp.int32, (128, 128), 1)
@@ -231,32 +269,43 @@
             table[pl.ds(pl.multiple_of(m * 128, 128), 128), :] = jnp.sin(angle + shift)
 
     phase_a(0)
+    phase_a(1)
     loads["hid"].wait()
-    head(0)
-    phase_a(1)
+    far_head(0)
+    phase_a(2)
+    phase_a(3)
+    pl.semaphore_wait(barrier, len(partners))
+    for j in range(4):
+        core_send(j)
+    far_send(0)
     phase_b(0)
-    head(1)
-    phase_a(2)
+    near_head(0, 0)
     phase_b(1)
-    head(2)
-    phase_a(3)
+    near_head(0, 1)
     phase_b(2)
-    head(4)
     phase_b(3)
+    up_exchange()
+    near_sum(0, 0)
+    near_sum(0, 1)
     phase_c(0)
-    head(5)
+    own_head(0)
     phase_c(1)
-    head(6)
-    up_exchange()
+    far_head(1)
     phase_c(2)
-    head(3)
     phase_c(3)
-    head(7)
+    far_send(1)
+    near_head(1, 0)
+    near_head(1, 1)
+    own_head(1)
     trig()
-
+    select_row = lax.broadcasted_iota(jnp.int32, (128, 512), 0)
+    select_col = lax.broadcasted_iota(jnp.int32, (128, 512), 1)
+    place = (select_row % 64) // 2 * 16 + select_row % 2 * 2
+    key_pick = jnp.where((select_row < 64) & (select_col == place), 1.0, 0.0)
+    value_pick = jnp.where((select_row >= 64) & (select_col == place + 1), 1.0, 0.0)
     for j in range(3):
-        await_recv(zr.at[j], z_r.at[j])
-    await_recv(zr.at[3, pl.ds(1, 7)], z_r.at[3])
+        await_bytes(zr.at[j], z_r.at[j])
+    await_bytes(zr.at[3, pl.ds(1, 7)], z_r.at[3])
     total = zs[3, t].astype(jnp.float32)
     for j in range(4):
         for k in range(8):
@@ -267,7 +316,7 @@
         loads[name].wait()
     new = adam_step(state[0], state[1], state[2], total[0:32], down_learning_rate)
     ab[chip, c, 0:32] = new[0].astype(jnp.bfloat16)
-    await_recv(up_all.at[pl.ds(0, 7)], u_r)
+    await_bytes(up_all.at[pl.ds(0, 7)], u_r)
     first, second = up_all[t // 2], up_all[4 + t // 2]
     odd = t % 2 == 1
 
@@ -287,68 +336,70 @@
     for k in range(1, 16):
         q = (chip + k) % 16
         send(ab.at[chip, c], ab.at[chip, c], a_s, a_r, (q * 2 + c, t))
+    sent.append((ab.at[pl.ds(0, 15), c], a_s))
     new_up = adam_step(
         up_state[0:4], up_state[8:12], up_state[16:20], total[32:36], rate_up
     )
-    outs = []
-    for n, ref in enumerate((new_p_down, new_m_down, new_v_down)):
+    for n in range(3):
         new_down_v[n] = new[n]
-        outs.append(pltpu.make_async_copy(new_down_v.at[n], ref, o_sem.at[n]))
-    for n, ref in enumerate((new_p_up, new_m_up, new_v_up)):
-        new_up_v[n] = new_up[n]
-        outs.append(pltpu.make_async_copy(new_up_v.at[n], ref, o_sem.at[3 + n]))
-    for cp in outs:
-        cp.start()
-
-    await_recv(ab.at[pl.ds(0, 15), c], a_r)
-    copies.append(send(ab.at[:, c], ab.at[:, c], f_s, f_r, (f_of(y, zl, 1 - c), t)))
+        new_up_v[n] = jnp.concatenate([new_up[n], new_up[n]], axis=0)
+    outs = [
+        pltpu.make_async_copy(new_down_v, new_down_h, o_sem.at[0]),
+        pltpu.make_async_copy(new_up_v, new_up_h, o_sem.at[1]),
+    ]
+    for move in outs:
+        move.start()
+
+    near_sum(1, 0)
+    near_sum(1, 1)
+    await_bytes(ab.at[pl.ds(0, 15), c], a_r)
+    send(ab.at[:, c], ab.at[:, c], f_s, f_r, (f_of(y, zl, 1 - c), t))
+    sent.append((ab.at[:, c], f_s))
     head_forward()
-    await_recv(ab.at[:, 1 - c], f_r)
+    await_bytes(ab.at[:, 1 - c], f_r)
 
     adapter = ab[:, :, 0:32].reshape(FEATURES, 128)
-    for k in (4, 5, 3, 6, 2, 7, 1, 0):
+    for m in range(2):
+        part = pl.ds(m * 384, 384)
+        hs[m * 4 : m * 4 + 4] = dot(hid[part, :], adapter).astype(jnp.bfloat16).reshape(4, 96, 128)
+    for k in (4, 5, 3, 6, 2, 7, 1):
         to_t = (t + k) % 8
-        part = pl.ds(pl.multiple_of(to_t * 96, 96), 96)
-        hs[to_t] = dot(hid[part, :], adapter).astype(jnp.bfloat16)
-        if k:
-            send(hs.at[to_t], hr.at[k - 1], hs_s, hs_r, (f, to_t))
-    select_row = lax.broadcasted_iota(jnp.int32, (128, 512), 0)
-    select_col = lax.broadcasted_iota(jnp.int32, (128, 512), 1)
-    place = (select_row % 64) // 2 * 16 + select_row % 2 * 2
-    key_pick = jnp.where((select_row < 64) & (select_col == place), 1.0, 0.0)
-    value_pick = jnp.where((select_row >= 64) & (select_col == place + 1), 1.0, 0.0)
+        send(hs.at[to_t], hr.at[k - 1], hs_s, hs_r, (f, to_t))
+    sent.append((hr, hs_s))
     rolls = ab[:, :, 32:48].reshape(512, 128)
     key_block = dot(key_pick.astype(jnp.bfloat16), rolls).astype(jnp.bfloat16)
     value_block = dot(value_pick.astype(jnp.bfloat16), rolls).astype(jnp.bfloat16)
 
-    await_recv(hr, hs_r)
+    await_bytes(hr, hs_r)
     mixed = hs[t].astype(jnp.float32)
     for k in range(7):
         mixed = mixed + hr[k].astype(jnp.float32)
     hall[t] = mixed.astype(jnp.bfloat16)
     for k in (4, 5, 3, 6, 2, 7, 1):
         send(hall.at[t], hall.at[t], hg_s, hg_r, (f, (t + k) % 8))
-
-    for s in range(3, 6):
-        await_recv(xr.at[s], x_r.at[s])
-    await_recv(zbr, b_r)
+    sent.append((hr, hg_s))
+
+    head_arrive(1)
+    await_bytes(zbr, b_r)
 
     @pl.loop(0, 6)
     def _(m):
         part = pl.ds(pl.multiple_of(m * 128, 128), 128)
         own_heads[1, part, :] = (
             own_heads[1, part, :]
-            + xr[3, part, :].astype(jnp.float32)
-            + xr[4, part, :].astype(jnp.float32)
-            + xr[5, part, :].astype(jnp.float32)
+            + xr[1, 0, part, :].astype(jnp.float32)
+            + xr[1, 1, part, :].astype(jnp.float32)
             + zbr[part, :].astype(jnp.float32)
         )
 
-    await_recv(hall.at[pl.ds(0, 7)], hg_r)
-    final = []
+    await_bytes(hall.at[pl.ds(0, 7)], hg_r)
     low = lax.broadcasted_iota(jnp.int32, (96, 128), 1) < 64
     for m in range(8):
         part = pl.ds(m * 96, 96)
+        if m == 4:
+            half_rows = pl.ds(0, 384)
+            outs.append(pltpu.make_async_copy(out_v.at[half_rows], out_h.at[half_rows], o_sem.at[2]))
+            outs[-1].start()
         rot = table[part, :]
         swapped = pltpu.roll(rot, 64, 1)
         cosine = jnp.where(low, rot, swapped)
@@ -357,21 +408,25 @@
         value = own_heads[1, part, 128:256] + adapter_scale * dot(hall[m], value_block)
         out_v[part, 0:128] = (key * cosine + pltpu.roll(key, 64, 1) * sine).astype(jnp.bfloat16)
         out_v[part, 128:256] = value.astype(jnp.bfloat16)
-    last = pltpu.make_async_copy(out_v, out, st_sem)
-    last.start()
-
-    for cp in copies:
-        cp.wait_send()
-    for j in range(3):
-        await_recv(zs.at[j], z_s.at[j])
-    await_recv(zs.at[3, pl.ds(1, 7)], z_s.at[3])
-    await_recv(up_all.at[pl.ds(0, 7)], u_s)
-    await_recv(ab.at[pl.ds(0, 15), c], a_s)
-    await_recv(hr, hs_s)
-    await_recv(hr, hg_s)
-    for cp in outs:
-        cp.wait()
-    last.wait()
+
+    half_rows = pl.ds(384, 384)
+    outs.append(pltpu.make_async_copy(out_v.at[half_rows], out_h.at[half_rows], o_sem.at[3]))
+    outs[-1].start()
+
+    for ref, sem in sent:
+        await_bytes(ref, sem)
+    for move in outs:
+        move.wait()
+
+
+def write_out(states, down, up, *refs):
+    outs, sem = refs[:7], refs[7]
+    parts = [states] + [down.at[n] for n in range(3)] + [up.at[n, pl.ds(0, 4)] for n in range(3)]
+    moves = [pltpu.make_async_copy(a, b, sem.at[n]) for n, (a, b) in enumerate(zip(parts, outs))]
+    for move in moves:
+        move.start()
+    for move in moves:
+        move.wait()
 
 
 def on_device(
@@ -384,11 +439,13 @@
     dma = pltpu.SemaphoreType.DMA
     results = pl.pallas_call(
         kernel,
-        out_shape=[jax.ShapeDtypeStruct((TOKENS_LOCAL, HEAD_COLUMNS), bf16)]
-        + [jax.ShapeDtypeStruct((32, 128), f32)] * 3
-        + [jax.ShapeDtypeStruct((4, 128), f32)] * 3,
+        out_shape=[
+            jax.ShapeDtypeStruct((TOKENS_LOCAL, HEAD_COLUMNS), bf16),
+            jax.ShapeDtypeStruct((3, 32, 128), f32),
+            jax.ShapeDtypeStruct((3, 8, 128), f32),
+        ],
         in_specs=[anywhere, anywhere, pl.BlockSpec(memory_space=pltpu.SMEM)] + [anywhere] * 8,
-        out_specs=[anywhere] * 7,
+        out_specs=[anywhere] * 3,
         scratch_shapes=[
             vm((TOKENS_LOCAL, FEATURES), bf16),
             vm((8, FEATURES, HEAD_COLUMNS), bf16),
@@ -403,8 +460,11 @@
             vm((8, 96, 128), bf16),
             vm((7, 96, 128), bf16),
             vm((8, 96, 128), bf16),
-            vm((6, TOKENS_LOCAL, HEAD_COLUMNS), bf16),
-            vm((6, TOKENS_LOCAL, HEAD_COLUMNS), bf16),
+            vm((2, TOKENS_LOCAL, HEAD_COLUMNS), bf16),
+            vm((2, 2, TOKENS_LOCAL // 2, HEAD_COLUMNS), bf16),
+            vm((2, TOKENS_LOCAL, HEAD_COLUMNS), f32),
+            vm((2, 2, TOKENS_LOCAL, HEAD_COLUMNS), bf16),
+            vm((2, 2, TOKENS_LOCAL, HEAD_COLUMNS), bf16),
             vm((2, TOKENS_LOCAL, HEAD_COLUMNS), f32),
             vm((TOKENS_LOCAL, HEAD_COLUMNS), bf16),
             vm((TOKENS_LOCAL, HEAD_COLUMNS), bf16),
@@ -412,9 +472,9 @@
             vm((3, 32, 128), f32),
             vm((24, 128), f32),
             vm((8, 24, 128), f32),
+            vm((TOKENS_LOCAL, HEAD_COLUMNS), bf16),
             vm((3, 32, 128), f32),
-            vm((3, 4, 128), f32),
-            vm((TOKENS_LOCAL, HEAD_COLUMNS), bf16),
+            vm((3, 8, 128), f32),
             dma((24,)),
             dma((4,)), dma((4,)),
             dma((4, 3)), dma((4, 3)),
@@ -423,11 +483,11 @@
             dma(()), dma(()),
             dma(()), dma(()),
             dma(()), dma(()),
-            dma((6,)), dma((6,)),
+            dma((2, 2)), dma((2, 2)),
+            dma((2, 2, 2)), dma((2, 2, 2)),
             dma(()), dma(()),
             dma(()), dma(()),
-            dma(()),
-            dma((6,)),
+            dma((4,)),
         ],
         compiler_params=pltpu.CompilerParams(
             collective_id=0, has_side_effects=True, vmem_limit_bytes=56 * 1024 * 1024
@@ -448,7 +508,15 @@
         first_up,
         second_up,
     )
-    states, p_down, m_down, v_down, p_up, m_up, v_up = results
+    states, p_down, m_down, v_down, p_up, m_up, v_up = pl.pallas_call(
+        write_out,
+        out_shape=[jax.ShapeDtypeStruct((TOKENS_LOCAL, HEAD_COLUMNS), bf16)]
+        + [jax.ShapeDtypeStruct((32, 128), f32)] * 3
+        + [jax.ShapeDtypeStruct((4, 128), f32)] * 3,
+        in_specs=[pl.BlockSpec(memory_space=vm)] * 3,
+        out_specs=[anywhere] * 7,
+        scratch_shapes=[dma((7,))],
+    )(*results)
     return (states, p_down[None], m_down[None], v_down[None], p_up, m_up, v_up)
 
 

time: 105 us -> 76.7 us (0.73)
  Pallas kernels: 94.1 us -> 75.1 us
  local copies, waits for them, and re-layouts: 9.49 us -> 0 us
    pallas_call x1, Pallas kernels: 94.1 us -> 73.2 us  [on_device(): pl.pallas_call(kernel, out_shape=[jax.ShapeDtypeStruct((TOKENS_LOCAL, HEA...]
    unnamed x7 -> x0, local copies, waits for them, and re-layouts: 9.49 us -> none
    pallas_call x0 -> x1, Pallas kernels: none -> 1.85 us  [on_device(): pl.pallas_call(write_out, out_shape=[jax.ShapeDtypeStruct((TOKENS_LOCAL,...]
where the time goes in v2:
time: 76.7 us; the launch traced here: 75.7 us
  Pallas kernels  75.1 us (98%)
    pallas_call x1, Pallas kernels, on_device(): pl.pallas_call(kernel, out_shape=[jax.ShapeDtypeStruct((TOKENS_LOCAL, HEA...  73.2 us
    pallas_call x1, Pallas kernels, on_device(): pl.pallas_call(write_out, out_shape=[jax.ShapeDtypeStruct((TOKENS_LOCAL,...  1.85 us

profile of v2, /device:TPU:8, one launch (start us, length us, event | category | flops | bytes accessed | tf_op | source)
XLA Modules:
  0.0 75.7 jit_solution(17469488722631924660)
XLA Ops:
  0.6 73.2 %shard_map.162 = (bf16[768,256]{1,0:T(8,128)(2,1)}, f32[3,32,128]{2,1,0:T(8,128)}, f32[3,8,128]{2,1,0:T(8,128)}) custom-call(bf16[768,1024]{1,0:T(8,128)(2,1)} %hidden.1, bf16[1024,2048]{1,0:T(8,128)(2,1)} %weight.1, s32[1,6]{1,0:T(1,128)} %lengths.1, f32[8,4,4,2,32,128]{5,4,3,2,1,0:T(8,128)} %bitcast.8, f32[4,4,2,32,128]{4,3,2,1,0:T(8,128)} %bitcast.9, ...), custom_call_target="tpu_custom_call" | custom-call | flops 3460300800 | bytes 12582912 | tf_op jit(solution)/shard_map/pallas_call | solution.py:440
  73.9 1.8 %shard_map.163 = (bf16[768,256]{1,0:T(8,128)(2,1)}, f32[32,128]{1,0:T(8,128)}, f32[32,128]{1,0:T(8,128)}, f32[32,128]{1,0:T(8,128)}, f32[4,128]{1,0:T(4,128)}, /*index=5*/f32[4,128]{1,0:T(4,128)}, f32[4,128]{1,0:T(4,128)}) custom-call(bf16[768,256]{1,0:T(8,128)(2,1)} %get-tuple-element.17.states, f32[3,32,128]{2,1,0:T(8,128)} %get-tuple-element.18.down, ...), custom_call_target="tpu_custom_call" | custom-call | tf_op jit(solution)/shard_map/pallas_call | solution.py:511

commit v3 on v2

--- a/solution.py
+++ b/solution.py
@@ -22,7 +22,7 @@
 adapter_scale = 2.0
 rope_base = 500000.0
 
-Z_STEPS = (2, 1, 3, 0)
+Z_STEPS = (1, 3, 2, 0)
 X_STEPS = (2, 1, 3, 0)
 
 
@@ -235,10 +235,11 @@
             await_bytes(xr.at[half, side, lower], x_r.at[half, side, 0])
             await_bytes(xr.at[half, side, upper], x_r.at[half, side, 1])
 
-    def head_forward():
-        head_arrive(0)
-
-        @pl.loop(0, 6)
+    def head_forward(h):
+        if h == 0:
+            head_arrive(0)
+
+        @pl.loop(3 * h, 3 * h + 3)
         def _(m):
             part = pl.ds(pl.multiple_of(m * 128, 128), 128)
             zbs[part, :] = (
@@ -247,8 +248,9 @@
                 + xr[0, 1, part, :].astype(jnp.float32)
             ).astype(jnp.bfloat16)
 
-        send(zbs, zbr, b_s, b_r, (f, (1 - zh) * 4 + x))
-        sent.append((zbs, b_s))
+        half_part = pl.ds(384 * h, 384)
+        send(zbs.at[half_part], zbr.at[half_part], b_s.at[h], b_r.at[h], (f, (1 - zh) * 4 + x))
+        sent.append((zbs.at[half_part], b_s.at[h]))
 
     def trig():
         lane = lax.broadcasted_iota(jnp.int32, (128, 128), 1)
@@ -303,6 +305,7 @@
     place = (select_row % 64) // 2 * 16 + select_row % 2 * 2
     key_pick = jnp.where((select_row < 64) & (select_col == place), 1.0, 0.0)
     value_pick = jnp.where((select_row >= 64) & (select_col == place + 1), 1.0, 0.0)
+    head_forward(0)
     for j in range(3):
         await_bytes(zr.at[j], z_r.at[j])
     await_bytes(zr.at[3, pl.ds(1, 7)], z_r.at[3])
@@ -355,14 +358,13 @@
     await_bytes(ab.at[pl.ds(0, 15), c], a_r)
     send(ab.at[:, c], ab.at[:, c], f_s, f_r, (f_of(y, zl, 1 - c), t))
     sent.append((ab.at[:, c], f_s))
-    head_forward()
     await_bytes(ab.at[:, 1 - c], f_r)
 
     adapter = ab[:, :, 0:32].reshape(FEATURES, 128)
     for m in range(2):
         part = pl.ds(m * 384, 384)
         hs[m * 4 : m * 4 + 4] = dot(hid[part, :], adapter).astype(jnp.bfloat16).reshape(4, 96, 128)
-    for k in (4, 5, 3, 6, 2, 7, 1):
+    for k in range(1, 8):
         to_t = (t + k) % 8
         send(hs.at[to_t], hr.at[k - 1], hs_s, hs_r, (f, to_t))
     sent.append((hr, hs_s))
@@ -370,17 +372,19 @@
     key_block = dot(key_pick.astype(jnp.bfloat16), rolls).astype(jnp.bfloat16)
     value_block = dot(value_pick.astype(jnp.bfloat16), rolls).astype(jnp.bfloat16)
 
+    head_forward(1)
     await_bytes(hr, hs_r)
     mixed = hs[t].astype(jnp.float32)
     for k in range(7):
         mixed = mixed + hr[k].astype(jnp.float32)
     hall[t] = mixed.astype(jnp.bfloat16)
-    for k in (4, 5, 3, 6, 2, 7, 1):
+    for k in range(1, 8):
         send(hall.at[t], hall.at[t], hg_s, hg_r, (f, (t + k) % 8))
     sent.append((hr, hg_s))
 
     head_arrive(1)
-    await_bytes(zbr, b_r)
+    await_bytes(zbr.at[pl.ds(0, 384)], b_r.at[0])
+    await_bytes(zbr.at[pl.ds(384, 384)], b_r.at[1])
 
     @pl.loop(0, 6)
     def _(m):
@@ -485,7 +489,7 @@
             dma(()), dma(()),
             dma((2, 2)), dma((2, 2)),
             dma((2, 2, 2)), dma((2, 2, 2)),
-            dma(()), dma(()),
+            dma((2,)), dma((2,)),
             dma(()), dma(()),
             dma((4,)),
         ],

time: 76.7 us -> 73.8 us (0.962)
  the two profiles are of different devices: /device:TPU:8 before, /device:TPU:70 now
where the time goes in v3:
time: 73.8 us; the launch traced here: 73.7 us
  Pallas kernels  73 us (99%)
    pallas_call x1, Pallas kernels, on_device(): pl.pallas_call(kernel, out_shape=[jax.ShapeDtypeStruct((TOKENS_LOCAL, HEA...  71.2 us
    pallas_call x1, Pallas kernels, on_device(): pl.pallas_call(write_out, out_shape=[jax.ShapeDtypeStruct((TOKENS_LOCAL,...  1.85 us

profile of v3, /device:TPU:70, one launch (start us, length us, event | category | flops | bytes accessed | tf_op | source)
XLA Modules:
  0.0 73.7 jit_solution(8229661589818373822)
XLA Ops:
  0.6 71.2 %shard_map.162 = (bf16[768,256]{1,0:T(8,128)(2,1)}, f32[3,32,128]{2,1,0:T(8,128)}, f32[3,8,128]{2,1,0:T(8,128)}) custom-call(bf16[768,1024]{1,0:T(8,128)(2,1)} %hidden.1, bf16[1024,2048]{1,0:T(8,128)(2,1)} %weight.1, s32[1,6]{1,0:T(1,128)} %lengths.1, f32[8,4,4,2,32,128]{5,4,3,2,1,0:T(8,128)} %bitcast.8, f32[4,4,2,32,128]{4,3,2,1,0:T(8,128)} %bitcast.9, ...), custom_call_target="tpu_custom_call" | custom-call | flops 3460300800 | bytes 12582912 | tf_op jit(solution)/shard_map/pallas_call | solution.py:444
  71.8 1.8 %shard_map.163 = (bf16[768,256]{1,0:T(8,128)(2,1)}, f32[32,128]{1,0:T(8,128)}, f32[32,128]{1,0:T(8,128)}, f32[32,128]{1,0:T(8,128)}, f32[4,128]{1,0:T(4,128)}, /*index=5*/f32[4,128]{1,0:T(4,128)}, f32[4,128]{1,0:T(4,128)}) custom-call(bf16[768,256]{1,0:T(8,128)(2,1)} %get-tuple-element.17.states, f32[3,32,128]{2,1,0:T(8,128)} %get-tuple-element.18.down, ...), custom_call_target="tpu_custom_call" | custom-call | tf_op jit(solution)/shard_map/pallas_call | solution.py:515
